TPU v7x, 32 devices: a whole 2x2x4 slice. The times are simulated.
32 devices in a mesh: node: 8 (over y, x, core), dev: 4 (over z).
Axes of the slice: x: 2, y: 2, z: 4, core: 2. Of those that a mesh axis runs over, the one named last changes fastest.
Arguments:
- tokens: bfloat16 [128, 4096], P('node', 'dev'), may hold values from -6 to 6
- routes: int32 [128, 8], P('node'), may hold values from 0 to 7, as said below
- gate_codes: int32 [128, 8], P('node'), may hold values from 1 to 65535
- w_gate: bfloat16 [8, 4096, 2048], P('node', None, 'dev'), may hold values from -0.09375 to 0.09375
- w_up: bfloat16 [8, 4096, 2048], P('node', None, 'dev'), may hold values from -0.09375 to 0.09375
- w_down: bfloat16 [8, 2048, 4096], P('node', 'dev'), may hold values from -0.125 to 0.125
- cotangent: bfloat16 [128, 4096], P('node', 'dev'), may hold values from -6 to 6
Outputs:
- layer_out: bfloat16 [128, 4096], P('node', 'dev')
- token_grad: bfloat16 [128, 4096], P('node', 'dev')
- down_grad: bfloat16 [8, 2048, 4096], P('node', 'dev')
Inputs may be any that keep to these rules, and one draw needn't show every extreme that they name: `routes`: each token names 8 different experts, taken from at most 4 groups of 4 consecutive experts. Among the 16 tokens of one block (one index of node), no expert is named by more than 16 tokens, and in every block some expert is named by exactly 16.
All inputs are finite; a program needn't handle non-finite values.
Results may differ from a plain program's by a relative error of at most 0.012.
Values may be sent and summed in bfloat16 or wider, within the bound.
A program may use at most 64 MiB of HBM per device.

v0:
```python
import jax
import jax.numpy as jnp
from jax import lax
from jax.sharding import PartitionSpec as P

TOP_GROUPS = 4
GROUP_SIZE = 4


exact_mode = lax.Precision.HIGHEST


def slot_layout(routes, gate_codes, experts, capacity):
    tokens_here = routes.shape[0]
    member = (routes[:, :, None] == jnp.arange(experts, dtype=jnp.int32)[None, None, :]).astype(
        jnp.float32
    )
    named_by = jnp.sum(member, axis=1)
    earlier = (jnp.arange(tokens_here)[:, None] > jnp.arange(tokens_here)[None, :]).astype(
        jnp.float32
    )
    before = jnp.dot(earlier, named_by, precision=exact_mode)
    placed = named_by[:, :, None] * (
        before[:, :, None] == jnp.arange(capacity).astype(jnp.float32)[None, None, :]
    ).astype(jnp.float32)
    weights = gate_codes.astype(jnp.float32) / 65536.0
    gating = jnp.sum(member * weights[:, :, None], axis=1)
    return (placed, gating)


def deliver(local_rows, build, fold, initial):
    whole_rows = lax.all_gather(local_rows, "dev", axis=1, tiled=True)
    arrived = lax.all_to_all(build(whole_rows), "node", split_axis=0, concat_axis=0, tiled=True)
    return fold(initial, arrived, 0)


def send_back(partial_value):
    shares = lax.psum_scatter(
        partial_value.astype(jnp.bfloat16), "dev", scatter_dimension=2, tiled=True
    )
    return lax.all_to_all(shares, "node", split_axis=0, concat_axis=0, tiled=True)


def on_device(tokens, routes, gate_codes, w_gate, w_up, w_down, cotangent):
    experts = lax.axis_size("node")
    groups = experts // GROUP_SIZE
    chosen_count = min(TOP_GROUPS, groups)
    capacity = tokens.shape[0] * chosen_count // groups
    placed, gating = slot_layout(routes, gate_codes, experts, capacity)
    place_low = placed.astype(jnp.bfloat16)
    weighted = placed * gating[:, :, None]
    gate_mat = w_gate[0]
    up_mat = w_up[0]
    down_mat = w_down[0]
    hidden_width = gate_mat.shape[1]

    def spread_tokens(payload):
        return jnp.einsum(
            "tep,tf->epf", place_low, payload, preferred_element_type=jnp.float32
        ).astype(jnp.bfloat16)

    def spread_cotangent(payload):
        return jnp.einsum(
            "tep,tf->epf", weighted, payload.astype(jnp.float32), precision=exact_mode
        ).astype(jnp.bfloat16)

    def project_in(totals, portion, offset):
        gate_next = jnp.einsum("epf,fh->eph", portion, gate_mat, preferred_element_type=jnp.float32)
        up_next = jnp.einsum("epf,fh->eph", portion, up_mat, preferred_element_type=jnp.float32)
        return (gate_next, up_next)

    empty_hidden = jnp.zeros((experts, capacity, hidden_width), jnp.float32)
    gate_pre, up_pre = deliver(tokens, spread_tokens, project_in, (empty_hidden, empty_hidden))
    squash = jax.nn.sigmoid(gate_pre)
    hidden = (gate_pre * squash * up_pre).astype(jnp.bfloat16)
    partial_value = jnp.einsum("eph,hf->epf", hidden, down_mat, preferred_element_type=jnp.float32)
    returned = send_back(partial_value)
    layer_out = jnp.einsum(
        "tep,epf->tf", weighted, returned.astype(jnp.float32), precision=exact_mode
    ).astype(jnp.bfloat16)

    def project_cotangent(totals, portion, offset):
        grad_next = jnp.einsum("epf,hf->eph", portion, down_mat, preferred_element_type=jnp.float32)
        block_grad = jnp.einsum("eph,epf->hf", hidden, portion, preferred_element_type=jnp.float32)
        return (grad_next, block_grad)

    empty_down = jnp.zeros((hidden_width, down_mat.shape[1]), jnp.float32)
    hidden_grad, down_total = deliver(
        cotangent, spread_cotangent, project_cotangent, (empty_hidden, empty_down)
    )
    gate_grad = (hidden_grad * up_pre * squash * (1.0 + gate_pre * (1.0 - squash))).astype(
        jnp.bfloat16
    )
    up_grad = (hidden_grad * gate_pre * squash).astype(jnp.bfloat16)
    partial_back = jnp.einsum(
        "eph,fh->epf", gate_grad, gate_mat, preferred_element_type=jnp.float32
    )
    partial_back = partial_back + jnp.einsum(
        "eph,fh->epf", up_grad, up_mat, preferred_element_type=jnp.float32
    )
    returned_back = send_back(partial_back)
    token_grad = jnp.einsum(
        "tep,epf->tf", placed, returned_back.astype(jnp.float32), precision=exact_mode
    ).astype(jnp.bfloat16)
    return (layer_out, token_grad, down_total.astype(jnp.bfloat16)[None])


def solution(mesh):
    in_specs = (
        P("node", "dev"),
        P("node", None),
        P("node", None),
        P("node", None, "dev"),
        P("node", None, "dev"),
        P("node", "dev", None),
        P("node", "dev"),
    )
    out_specs = (P("node", "dev"), P("node", "dev"), P("node", "dev", None))
    return jax.shard_map(
        on_device, mesh=mesh, in_specs=in_specs, out_specs=out_specs, check_vma=False
    )
```

profile of v0, /device:TPU:0, one launch (start us, length us, event | category | flops | bytes accessed | tf_op | source)
XLA Modules:
  0.0 132.5 jit_solution(16287439819941731388)
XLA Ops:
  7.2 0.7 convert_multiply_fusion
  7.9 0.7 select_reduce_fusion
  8.6 0.1 fusion.38
  8.7 15.3 %all_gather.6 = bf16[16,4096]{1,0:T(8,128)(2,1)S(1)} all-gather(bf16[16,1024]{1,0:T(8,128)(2,1)} %param.7), channel_id=1, replica_groups=mesh['node'=8,'dev'=4] {'dev'}, dimensions={1}, use_global_device_ids=true | all-gather | bytes 163840 | tf_op jit(solution)/shard_map/all_gather | solution.py:32
  24.0 1.5 %convolution_convert_fusion.2 = bf16[8,16,4096]{2,1,0:T(8,128)(2,1)} fusion(bf16[16,4096]{1,0:T(8,128)(2,1)S(1)} %all_gather.6, f32[16,8]{0,1:T(8,128)S(1)} %get-tuple-element.4, f32[16]{0:T(128)S(1)} %iota_convert_fusion, f32[16,8]{0,1:T(8,128)S(1)} %fusion.38), kind=kOutput, calls=%fused_computation.6 | convolution fusion | flops 17305600 | bytes 1180736 | tf_op jit(solution)/shard_map/tep,tf->epf/dot_general | solution.py:58
  25.5 3.7 %all-to-all-start = ((bf16[8,16,4096]{2,1,0:T(8,128)(2,1)}), bf16[8,16,4096]{2,1,0:T(8,128)(2,1)S(1)}, u32[]{:S(2)}, u32[]{:S(2)}) async-start(bf16[8,16,4096]{2,1,0:T(8,128)(2,1)} %convolution_convert_fusion.2), calls=%async_computation | async-start | bytes 2097152 | tf_op jit(solution)/shard_map/all_to_all | solution.py:33
  29.2 13.7 %all_gather.7 = bf16[16,4096]{1,0:T(8,128)(2,1)S(1)} all-gather(bf16[16,1024]{1,0:T(8,128)(2,1)} %param.13), channel_id=1, replica_groups=mesh['node'=8,'dev'=4] {'dev'}, dimensions={1}, use_global_device_ids=true | all-gather | bytes 163840 | tf_op jit(solution)/shard_map/all_gather | solution.py:32
  42.8 2.1 %convolution_convert_fusion = bf16[8,16,4096]{2,1,0:T(8,128)(2,1)} fusion(bf16[16,4096]{1,0:T(8,128)(2,1)S(1)} %all_gather.7, f32[16,8]{0,1:T(8,128)S(1)} %get-tuple-element.3, f32[16,8]{0,1:T(8,128)S(1)} %get-tuple-element.4, f32[16]{0:T(128)S(1)} %iota_convert_fusion, f32[16,8]{0,1:T(8,128)S(1)} %fusion.38), kind=kOutput, calls=%fused_computation.4 | convolution fusion | flops 101193728 | bytes 1181248 | tf_op jit(solution)/shard_map/tep,tf->epf/dot_general | solution.py:63
  44.9 4.1 %all-to-all-start.2 = ((bf16[8,16,4096]{2,1,0:T(8,128)(2,1)}), bf16[8,16,4096]{2,1,0:T(8,128)(2,1)S(1)}, u32[]{:S(2)}, u32[]{:S(2)}) async-start(bf16[8,16,4096]{2,1,0:T(8,128)(2,1)} %convolution_convert_fusion), calls=%async_computation.3 | async-start | bytes 2097152 | tf_op jit(solution)/shard_map/all_to_all | solution.py:33
  49.0 0.0 reduce-scatter.3.cloned.1.call-start
  49.1 0.0 copy-start.2
  49.1 3.1 %fusion.10 = f32[8,16,512]{2,1,0:T(8,128)S(1)} fusion(bf16[8,16,4096]{2,1,0:T(8,128)(2,1)S(1)} %all-to-all-done, bf16[1,4096,512]{2,1,0:T(8,128)(2,1)} %param.10), kind=kOutput, calls=%fused_computation.15 | convolution fusion | flops 536870912 | bytes 5505024 | tf_op jit(solution)/shard_map/epf,fh->eph/dot_general | solution.py:68
  52.1 0.4 copy-done.2
  52.5 0.8 multiply_convert_fusion.2
  53.3 1.4 %copy-done = bf16[1,512,4096]{2,1,0:T(8,128)(2,1)S(1)} copy-done((bf16[1,512,4096]{2,1,0:T(8,128)(2,1)S(1)}, bf16[1,512,4096]{2,1,0:T(8,128)(2,1)}, u32[]{:S(2)}) %copy-start) | copy-done | bytes 4194328
  54.7 1.7 %convolution_convert_fusion.1 = bf16[8,16,4096]{2,1,0:T(8,128)(2,1)} fusion(bf16[8,16,512]{2,1,0:T(8,128)(2,1)S(1)} %get-tuple-element.5, bf16[1,512,4096]{2,1,0:T(8,128)(2,1)S(1)} %copy-done), kind=kOutput, calls=%fused_computation.5 | convolution fusion | flops 537395200 | bytes 5373952 | tf_op jit(solution)/shard_map/eph,hf->epf/dot_general | solution.py:76
  56.4 0.0 reduce-scatter.3.cloned.1.call-update
  56.5 0.0 reduce-scatter.5.cloned.1.call-start
  56.5 7.9 %all-to-all-done.2 = bf16[8,16,4096]{2,1,0:T(8,128)(2,1)S(1)} async-done(((bf16[8,16,4096]{2,1,0:T(8,128)(2,1)}), bf16[8,16,4096]{2,1,0:T(8,128)(2,1)S(1)}, u32[]{:S(2)}, u32[]{:S(2)}) %all-to-all-start.2) | async-done | bytes 1048608 | tf_op jit(solution)/shard_map/all_to_all | solution.py:33
  64.4 3.9 %fusion.2 = f32[8,16,512]{2,1,0:T(8,128)S(1)} fusion(bf16[8,16,4096]{2,1,0:T(8,128)(2,1)S(1)} %all-to-all-done.2, bf16[1,512,4096]{2,1,0:T(8,128)(2,1)} %param.12), kind=kOutput, calls=%fused_computation.7 | convolution fusion | flops 536870912 | bytes 5505024 | tf_op jit(solution)/shard_map/epf,hf->eph/dot_general | solution.py:83
  68.3 1.5 %fusion.8 = f32[8,16,4096]{2,1,0:T(8,128)S(1)} fusion(bf16[1,4096,512]{2,1,0:T(8,128)(2,1)S(1)} %copy-done.1, f32[8,16,512]{2,1,0:T(8,128)S(1)} %fusion.10, f32[8,16,512]{2,1,0:T(8,128)S(1)} %fusion.2, f32[8,16,512]{2,1,0:T(8,128)S(1)} %get-tuple-element.6), kind=kOutput, calls=%fused_computation.13 | convolution fusion | flops 537526272 | bytes 7077888 | tf_op jit(solution)/shard_map/eph,fh->epf/dot_general | solution.py:95
  69.8 0.7 copy-done.3
  70.5 2.5 %fusion.1 = bf16[8,16,4096]{2,1,0:T(8,128)(2,1)} fusion(f32[8,16,4096]{2,1,0:T(8,128)S(1)} %fusion.8, bf16[1,4096,512]{2,1,0:T(8,128)(2,1)S(1)} %copy-done.3, f32[8,16,512]{2,1,0:T(8,128)S(1)} %fusion.2, f32[8,16,512]{2,1,0:T(8,128)S(1)} %fusion.10), kind=kOutput, calls=%fused_computation.3 | convolution fusion | flops 538312704 | bytes 7864320 | tf_op jit(solution)/shard_map/eph,fh->epf/dot_general | solution.py:98
  73.0 0.0 reduce-scatter.5.cloned.1.call-update
  73.0 12.7 %reduce-scatter.3.cloned.1.call-done = bf16[8,16,1024]{2,1,0:T(8,128)(2,1)} async-done(((bf16[8,16,4096]{2,1,0:T(8,128)(2,1)}), bf16[8,16,1024]{2,1,0:T(8,128)(2,1)}) %reduce-scatter.3.cloned.1.call-update) | async-done | bytes 262160 | tf_op jit(solution)/shard_map/reduce_scatter | solution.py:38
  85.7 3.6 %all-to-all-start.1 = ((bf16[8,16,1024]{2,1,0:T(8,128)(2,1)}), bf16[8,16,1024]{2,1,0:T(8,128)(2,1)S(1)}, u32[]{:S(2)}, u32[]{:S(2)}) async-start(bf16[8,16,1024]{2,1,0:T(8,128)(2,1)} %reduce-scatter.3.cloned.1.call-done), calls=%async_computation.2 | async-start | bytes 524288 | tf_op jit(solution)/shard_map/all_to_all | solution.py:41
  89.3 3.3 %fusion = bf16[1,512,4096]{2,1,0:T(8,128)(2,1)} fusion(bf16[8,16,512]{2,1,0:T(8,128)(2,1)S(1)} %get-tuple-element.5, bf16[8,16,4096]{2,1,0:T(8,128)(2,1)S(1)} %all-to-all-done.2), kind=kOutput, calls=%fused_computation.1 | convolution fusion | flops 538968064 | bytes 5373952 | tf_op jit(solution)/shard_map/eph,epf->hf/dot_general | solution.py:84
  92.6 21.3 %reduce-scatter.5.cloned.1.call-done = bf16[8,16,1024]{2,1,0:T(8,128)(2,1)} async-done(((bf16[8,16,4096]{2,1,0:T(8,128)(2,1)}), bf16[8,16,1024]{2,1,0:T(8,128)(2,1)}) %reduce-scatter.5.cloned.1.call-update) | async-done | bytes 262160 | tf_op jit(solution)/shard_map/reduce_scatter | solution.py:38
  113.9 3.6 %all-to-all-start.3 = ((bf16[8,16,1024]{2,1,0:T(8,128)(2,1)}), bf16[8,16,1024]{2,1,0:T(8,128)(2,1)S(1)}, u32[]{:S(2)}, u32[]{:S(2)}) async-start(bf16[8,16,1024]{2,1,0:T(8,128)(2,1)} %reduce-scatter.5.cloned.1.call-done), calls=%async_computation.5 | async-start | bytes 524288 | tf_op jit(solution)/shard_map/all_to_all | solution.py:41
  117.6 1.1 fusion.12
  118.7 5.8 %all-to-all-done.3 = bf16[8,16,1024]{2,1,0:T(8,128)(2,1)S(1)} async-done(((bf16[8,16,1024]{2,1,0:T(8,128)(2,1)}), bf16[8,16,1024]{2,1,0:T(8,128)(2,1)S(1)}, u32[]{:S(2)}, u32[]{:S(2)}) %all-to-all-start.3) | async-done | bytes 262176 | tf_op jit(solution)/shard_map/all_to_all | solution.py:41
  124.5 1.1 fusion.13
  (7 shorter events, 0.0 us)
Async XLA Ops:
  25.5 19.5 %all-to-all-start = ((bf16[8,16,4096]{2,1,0:T(8,128)(2,1)}), bf16[8,16,4096]{2,1,0:T(8,128)(2,1)S(1)}, u32[]{:S(2)}, u32[]{:S(2)}) async-start(bf16[8,16,4096]{2,1,0:T(8,128)(2,1)} %convolution_convert_fusion.2), calls=%async_computation | async-start | bytes 2097152 | tf_op jit(solution)/shard_map/all_to_all | solution.py:33
  44.9 19.5 %all-to-all-start.2 = ((bf16[8,16,4096]{2,1,0:T(8,128)(2,1)}), bf16[8,16,4096]{2,1,0:T(8,128)(2,1)S(1)}, u32[]{:S(2)}, u32[]{:S(2)}) async-start(bf16[8,16,4096]{2,1,0:T(8,128)(2,1)} %convolution_convert_fusion), calls=%async_computation.3 | async-start | bytes 2097152 | tf_op jit(solution)/shard_map/all_to_all | solution.py:33
  49.0 36.7 %reduce-scatter.3.cloned.1.call-start = ((), (), s32[]{:S(2)}) async-start(), calls=%async_computation.6 | async-start | bytes 1310720 | tf_op jit(solution)/shard_map/reduce_scatter | solution.py:38
  49.1 3.5 %copy-start.2 = (bf16[1,4096,512]{2,1,0:T(8,128)(2,1)S(1)}, bf16[1,4096,512]{2,1,0:T(8,128)(2,1)}, u32[]{:S(2)}) copy-start(bf16[1,4096,512]{2,1,0:T(8,128)(2,1)} %param.11) | copy-start | bytes 12582916
  52.5 2.2 %copy-start = (bf16[1,512,4096]{2,1,0:T(8,128)(2,1)S(1)}, bf16[1,512,4096]{2,1,0:T(8,128)(2,1)}, u32[]{:S(2)}) copy-start(bf16[1,512,4096]{2,1,0:T(8,128)(2,1)} %param.12) | copy-start | bytes 12582916
  56.5 57.5 %reduce-scatter.5.cloned.1.call-start = ((), (), s32[]{:S(2)}) async-start(), calls=%async_computation.7 | async-start | bytes 1310720 | tf_op jit(solution)/shard_map/reduce_scatter | solution.py:38
  64.4 3.9 %copy-start.1 = (bf16[1,4096,512]{2,1,0:T(8,128)(2,1)S(1)}, bf16[1,4096,512]{2,1,0:T(8,128)(2,1)}, u32[]{:S(2)}) copy-start(bf16[1,4096,512]{2,1,0:T(8,128)(2,1)} %param.10) | copy-start | bytes 12582916
  68.3 2.2 %copy-start.3 = (bf16[1,4096,512]{2,1,0:T(8,128)(2,1)S(1)}, bf16[1,4096,512]{2,1,0:T(8,128)(2,1)}, u32[]{:S(2)}) copy-start(bf16[1,4096,512]{2,1,0:T(8,128)(2,1)} %param.11) | copy-start | bytes 12582916
  85.7 28.2 %all-to-all-start.1 = ((bf16[8,16,1024]{2,1,0:T(8,128)(2,1)}), bf16[8,16,1024]{2,1,0:T(8,128)(2,1)S(1)}, u32[]{:S(2)}, u32[]{:S(2)}) async-start(bf16[8,16,1024]{2,1,0:T(8,128)(2,1)} %reduce-scatter.3.cloned.1.call-done), calls=%async_computation.2 | async-start | bytes 524288 | tf_op jit(solution)/shard_map/all_to_all | solution.py:41
  113.9 10.6 %all-to-all-start.3 = ((bf16[8,16,1024]{2,1,0:T(8,128)(2,1)}), bf16[8,16,1024]{2,1,0:T(8,128)(2,1)S(1)}, u32[]{:S(2)}, u32[]{:S(2)}) async-start(bf16[8,16,1024]{2,1,0:T(8,128)(2,1)} %reduce-scatter.5.cloned.1.call-done), calls=%async_computation.5 | async-start | bytes 524288 | tf_op jit(solution)/shard_map/all_to_all | solution.py:41
Sparse Core Ops, SparseCore 0:
  56.6 29.0 reduce-scatter.2
  88.1 25.7 reduce-scatter.4
where the time goes:
time: 133 us; the launch traced here: 132 us
  waiting for transfers between devices  47.7 us (36%)
  blocking collectives  28.9 us (22%)
  matrix products  22.7 us (17%)
  starting transfers between devices  15.2 us (11%)
  between operations  14.1 us (11%)
  local copies, waits for them, and re-layouts  2.48 us (2%)
  other arithmetic  1.4 us (1%)
    reduce_scatter x2, waiting for transfers between devices, send_back(): lax.psum_scatter(partial_value.astype(jnp.bfloat16), 'dev', scatter_dimen...  34 us
    all_gather x2, blocking collectives, deliver(): whole_rows = lax.all_gather(local_rows, 'dev', axis=1, tiled=True)  28.9 us
    all_to_all x2, waiting for transfers between devices, deliver(): lax.all_to_all(build(whole_rows), 'node', split_axis=0, concat_axis=0, ti...  7.91 us
    all_to_all x2, starting transfers between devices, deliver(): lax.all_to_all(build(whole_rows), 'node', split_axis=0, concat_axis=0, ti...  7.81 us
    all_to_all x2, starting transfers between devices, send_back(): lax.all_to_all(shares, 'node', split_axis=0, concat_axis=0, tiled=True)  7.29 us
    all_to_all x2, waiting for transfers between devices, send_back(): lax.all_to_all(shares, 'node', split_axis=0, concat_axis=0, tiled=True)  5.79 us
    dot_general x1, matrix products, project_cotangent(): jnp.einsum('epf,hf->eph', portion, down_mat, preferred_element_type=jnp.f...  3.88 us
    dot_general x1, matrix products, project_cotangent(): jnp.einsum('eph,epf->hf', hidden, portion, preferred_element_type=jnp.flo...  3.29 us
  transfers between devices with their start and end apart: 6, of which 4 were waited for; matrix products, arithmetic and copies ran while one was open for 15% of the time, Pallas kernels for 0%

commit v1 on v0

--- a/solution.py
+++ b/solution.py
@@ -1,10 +1,310 @@
 import jax
 import jax.numpy as jnp
 from jax import lax
+from jax.experimental import pallas as pl
+from jax.experimental.pallas import tpu as pltpu
 from jax.sharding import PartitionSpec as P
 
 TOP_GROUPS = 4
 GROUP_SIZE = 4
+MESH_IDS = pl.DeviceIdType.MESH
+ORDER_IN = (0, 1, 3, 2)
+ORDER_OUT = (2, 1, 3, 0)
+
+
+def dot(a, b, a_dim=1, b_dim=0):
+    return lax.dot_general(
+        a, b, (((a_dim,), (b_dim,)), ((), ())), preferred_element_type=jnp.float32
+    )
+
+
+def fused_kernel(
+    tok_in, routes_in, codes_in, wg_in, wu_in, wd_in, cot_in,
+    layer_out, token_grad, down_out,
+    x_all, gates, wg, wu, wd, gate_pre, up_pre, hid_grad, hidden, wcot, gate_grad, up_grad,
+    part, r1, s1, r2, s2, r3, s3, r4, dgrad,
+    in_send, in_recv, g_send, g_recv, out_send, out_recv, w_sem, own_sem, d_sem,
+):
+    node, d = lax.axis_index("node"), lax.axis_index("dev")
+    y, x, c = node // 4, (node // 2) % 2, node % 2
+    x_peer = (y * 2 + 1 - x) * 2 + c
+    y_peer = ((1 - y) * 2 + x) * 2 + c
+    c_peer = (y * 2 + x) * 2 + 1 - c
+    width = tok_in.shape[1]
+    rows = 8 * tok_in.shape[0]
+    sent = []
+
+    def send(src, dst, send_sem, recv_sem, target):
+        copy = pltpu.make_async_remote_copy(
+            src_ref=src, dst_ref=dst, send_sem=send_sem, recv_sem=recv_sem,
+            device_id=target, device_id_type=MESH_IDS,
+        )
+        copy.start()
+        sent.append(copy)
+        return copy
+
+    def column(k):
+        return pl.ds(pl.multiple_of(((d + k) % 4) * width, width), width)
+
+    barrier = pltpu.get_barrier_semaphore()
+    peers = [(x_peer, d), (y_peer, d), (c_peer, d)] + [(node, (d + j) % 4) for j in (1, 2, 3)]
+    for peer in peers:
+        pl.semaphore_signal(barrier, inc=1, device_id=peer, device_id_type=MESH_IDS)
+
+    loads = {}
+    for k in ORDER_IN:
+        loads["g", k] = pltpu.make_async_copy(wg_in.at[0, column(k)], wg.at[k], w_sem.at[0, k])
+        loads["u", k] = pltpu.make_async_copy(wu_in.at[0, column(k)], wu.at[k], w_sem.at[1, k])
+    for k in range(4):
+        loads["d", k] = pltpu.make_async_copy(
+            wd_in.at[0, :, column(k)], wd.at[k], w_sem.at[2, k]
+        )
+    for load in loads.values():
+        load.start()
+
+    lane = lax.broadcasted_iota(jnp.int32, (tok_in.shape[0], 128), 1)
+    table = jnp.zeros((tok_in.shape[0], 128), jnp.float32)
+    for j in range(routes_in.shape[1]):
+        table = table + jnp.where(
+            routes_in[:, j : j + 1] == lane,
+            codes_in[:, j : j + 1].astype(jnp.float32) / 65536.0,
+            0.0,
+        )
+    gates[y, x, c] = table
+    x_all[0, 0, y, x, c] = tok_in[...]
+    x_all[1, 0, y, x, c] = cot_in[...]
+
+    pl.semaphore_wait(barrier, 6)
+
+    z_hop = {}
+
+    def start_z(a):
+        own = tok_in if a == 0 else cot_in
+        for j in (1, 3, 2):
+            z_hop[a, 4 - j] = send(
+                own, x_all.at[a, 4 - j, y, x, c], in_send.at[a, j, 0], in_recv.at[a, 4 - j, 0],
+                (node, (d + j) % 4),
+            )
+
+    hop = {}
+
+    def gather_stage(block, stage):
+        a, i = divmod(block, 4)
+        k = ORDER_IN[i]
+        x_first = i % 2 == 0
+        if stage == 0:
+            if k:
+                z_hop[a, k].wait_recv()
+            ref = x_all.at[a, k, y, x, c]
+            target = x_peer if x_first else y_peer
+        else:
+            hop[a, k].wait_recv()
+            if stage == 1 and x_first:
+                ref, target = x_all.at[a, k, y, :, c], y_peer
+            elif stage == 1:
+                ref, target = x_all.at[a, k, :, x, c], x_peer
+            elif stage == 2:
+                ref, target = x_all.at[a, k, :, :, c], c_peer
+            else:
+                return
+        hop[a, k] = send(
+            ref, ref, in_send.at[a, k, stage + 1], in_recv.at[a, k, stage + 1], (target, d)
+        )
+
+    def gates_stage(stage):
+        if stage:
+            hop["gates"].wait_recv()
+        if stage < 3:
+            ref, target = (
+                (gates.at[y, x, c], x_peer),
+                (gates.at[y, :, c], y_peer),
+                (gates.at[:, :, c], c_peer),
+            )[stage]
+            hop["gates"] = send(ref, ref, g_send.at[stage], g_recv.at[stage], (target, d))
+
+    def own_gates():
+        table = gates[...].reshape(rows, 128)
+        mine = lax.broadcasted_iota(jnp.int32, (rows, 128), 1) == node
+        return jnp.sum(jnp.where(mine, table, 0.0), axis=1, keepdims=True)
+
+    def project_in(i):
+        k = ORDER_IN[i]
+        lhs = x_all[0, k].reshape(rows, width)
+        for name, weight, total in (("g", wg, gate_pre), ("u", wu, up_pre)):
+            loads[name, k].wait()
+            product = dot(lhs, weight[k])
+            if i == 0:
+                total[...] = product
+            else:
+                total[...] += product
+
+    def make_hidden():
+        pre = gate_pre[...]
+        hidden[...] = (pre * jax.nn.sigmoid(pre) * up_pre[...]).astype(jnp.bfloat16)
+        for k in range(4):
+            loads["d", k].wait()
+
+    def project_cotangent(i):
+        k = ORDER_IN[i]
+        values = x_all[1, k].reshape(rows, width).astype(jnp.float32)
+        wcot[k] = (own_gates() * values).astype(jnp.bfloat16)
+        product = dot(wcot[k], wd[k], 1, 1)
+        if i == 0:
+            hid_grad[...] = product
+        else:
+            hid_grad[...] += product
+
+    def make_grads():
+        pre, grad = gate_pre[...], hid_grad[...]
+        q = jax.nn.sigmoid(pre)
+        gate_grad[...] = (grad * up_pre[...] * q * (1.0 + pre * (1.0 - q))).astype(jnp.bfloat16)
+        up_grad[...] = (grad * pre * q).astype(jnp.bfloat16)
+
+    back = {}
+
+    def add(one, other):
+        return (one.astype(jnp.float32) + other.astype(jnp.float32)).astype(jnp.bfloat16)
+
+    def return_stage(block, stage):
+        b, i = divmod(block, 4)
+        k = ORDER_OUT[i]
+        x_first = i % 2 == 0
+        if stage == 0:
+            if b == 0:
+                value = own_gates() * dot(hidden[...], wd[k])
+            else:
+                value = dot(gate_grad[...], wg[k], 1, 1) + dot(up_grad[...], wu[k], 1, 1)
+            part[b, k] = value.astype(jnp.bfloat16).reshape(part.shape[2:])
+            src, dst, target = part.at[b, k, :, :, 1 - c], r1.at[b, k], c_peer
+        elif stage == 1:
+            back[b, k].wait_recv()
+            s1[b, k] = add(part[b, k, :, :, c], r1[b, k])
+            if x_first:
+                src, target = s1.at[b, k, :, 1 - x], x_peer
+            else:
+                src, target = s1.at[b, k, 1 - y], y_peer
+            dst = r2.at[b, k]
+        elif stage == 2:
+            back[b, k].wait_recv()
+            s2[b, k] = add(s1[b, k, :, x] if x_first else s1[b, k, y], r2[b, k])
+            if x_first:
+                src, target = s2.at[b, k, 1 - y], y_peer
+            else:
+                src, target = s2.at[b, k, 1 - x], x_peer
+            dst = r3.at[b, k]
+        else:
+            back[b, k].wait_recv()
+            s3[b, k] = add(s2[b, k, y] if x_first else s2[b, k, x], r3[b, k])
+            if k:
+                back[b, "z", 4 - k] = send(
+                    s3.at[b, k], r4.at[b, 4 - k], out_send.at[b, k, 3], out_recv.at[b, 4 - k, 3],
+                    (node, (d + k) % 4),
+                )
+            return
+        back[b, k] = send(
+            src, dst, out_send.at[b, k, stage], out_recv.at[b, k, stage], (target, d)
+        )
+
+    def finish(b, result):
+        total = s3[b, 0].astype(jnp.float32)
+        for k in (1, 3, 2):
+            back[b, "z", k].wait_recv()
+            total = total + r4[b, k].astype(jnp.float32)
+        result[...] = total.astype(jnp.bfloat16)
+
+    stores = []
+
+    def down_block(k):
+        dgrad[k] = dot(hidden[...], wcot[k], 0, 0).astype(jnp.bfloat16)
+        store = pltpu.make_async_copy(dgrad.at[k], down_out.at[0, :, column(k)], d_sem.at[k])
+        store.start()
+        stores.append(store)
+
+    start_z(0)
+    gates_stage(0)
+    for slot in range(18):
+        for stage in (3, 2, 1, 0):
+            if 0 <= slot - stage < 8:
+                gather_stage(slot - stage, stage)
+        if slot == 0:
+            start_z(1)
+        if 1 <= slot <= 3:
+            gates_stage(slot)
+        for stage in (3, 2, 1):
+            if 0 <= slot - 7 - stage < 8:
+                return_stage(slot - 7 - stage, stage)
+        if 3 <= slot <= 6:
+            project_in(slot - 3)
+        if slot == 6:
+            make_hidden()
+        if 7 <= slot <= 14:
+            return_stage(slot - 7, 0)
+        if 7 <= slot <= 10:
+            project_cotangent(slot - 7)
+        if slot == 10:
+            make_grads()
+        if slot >= 14:
+            down_block(slot - 14)
+        if slot == 15:
+            finish(0, layer_out)
+    finish(1, token_grad)
+    for copy in sent:
+        copy.wait_send()
+    for store in stores:
+        store.wait()
+
+
+def fused(tokens, routes, gate_codes, w_gate, w_up, w_down, cotangent):
+    here, width = tokens.shape
+    hidden_width = w_gate.shape[2]
+    rows = 8 * here
+    low, full = jnp.bfloat16, jnp.float32
+    vmem = pl.BlockSpec(memory_space=pltpu.VMEM)
+    anywhere = pl.BlockSpec(memory_space=pl.ANY)
+    dma = pltpu.SemaphoreType.DMA
+    scratch = [
+        pltpu.VMEM((2, 4, 2, 2, 2, here, width), low),
+        pltpu.VMEM((2, 2, 2, here, 128), full),
+        pltpu.VMEM((4, width, hidden_width), low),
+        pltpu.VMEM((4, width, hidden_width), low),
+        pltpu.VMEM((4, hidden_width, width), low),
+        pltpu.VMEM((rows, hidden_width), full),
+        pltpu.VMEM((rows, hidden_width), full),
+        pltpu.VMEM((rows, hidden_width), full),
+        pltpu.VMEM((rows, hidden_width), low),
+        pltpu.VMEM((4, rows, width), low),
+        pltpu.VMEM((rows, hidden_width), low),
+        pltpu.VMEM((rows, hidden_width), low),
+        pltpu.VMEM((2, 4, 2, 2, 2, here, width), low),
+        pltpu.VMEM((2, 4, 2, 2, here, width), low),
+        pltpu.VMEM((2, 4, 2, 2, here, width), low),
+        pltpu.VMEM((2, 4, 2, here, width), low),
+        pltpu.VMEM((2, 4, 2, here, width), low),
+        pltpu.VMEM((2, 4, here, width), low),
+        pltpu.VMEM((2, 4, here, width), low),
+        pltpu.VMEM((2, 4, here, width), low),
+        pltpu.VMEM((4, hidden_width, width), low),
+        dma((2, 4, 4)), dma((2, 4, 4)), dma((3,)), dma((3,)), dma((2, 4, 4)), dma((2, 4, 4)),
+        dma((3, 4)), dma((2,)), dma((4,)),
+    ]
+    flops = 2 * 7 * rows * 4 * width * hidden_width
+    return pl.pallas_call(
+        fused_kernel,
+        out_shape=(
+            jax.ShapeDtypeStruct(tokens.shape, low),
+            jax.ShapeDtypeStruct(tokens.shape, low),
+            jax.ShapeDtypeStruct(w_down.shape, low),
+        ),
+        in_specs=[vmem, vmem, vmem, anywhere, anywhere, anywhere, vmem],
+        out_specs=(vmem, vmem, anywhere),
+        scratch_shapes=scratch,
+        compiler_params=pltpu.CompilerParams(
+            collective_id=0, has_side_effects=True, vmem_limit_bytes=48 * 1024 * 1024
+        ),
+        cost_estimate=pl.CostEstimate(
+            flops=flops, bytes_accessed=8 * w_gate.size, transcendentals=2 * rows * hidden_width
+        ),
+    )(tokens, routes, gate_codes, w_gate, w_up, w_down, cotangent)
 
 
 exact_mode = lax.Precision.HIGHEST
@@ -116,6 +416,13 @@
         P("node", "dev"),
     )
     out_specs = (P("node", "dev"), P("node", "dev"), P("node", "dev", None))
+    nodes, devs = mesh.shape["node"], mesh.shape["dev"]
+
+    def body(tokens, routes, *rest):
+        every = routes.shape[1] == nodes
+        layer = fused if every and nodes == 8 and devs == 4 else on_device
+        return layer(tokens, routes, *rest)
+
     return jax.shard_map(
-        on_device, mesh=mesh, in_specs=in_specs, out_specs=out_specs, check_vma=False
-    )
+        body, mesh=mesh, in_specs=in_specs, out_specs=out_specs, check_vma=False
+    )

time: 133 us -> 75.3 us (0.57)
  Pallas kernels: 0 us -> 68.1 us
  waiting for transfers between devices: 47.7 us -> 0 us
  blocking collectives: 28.9 us -> 0 us
  matrix products: 22.7 us -> 0 us
  starting transfers between devices: 15.2 us -> 0 us
  between operations: 14.1 us -> 0.64 us
  local copies, waits for them, and re-layouts: 2.48 us -> 6.27 us
  other arithmetic: 1.4 us -> 0 us
    pallas_call x0 -> x1, Pallas kernels: none -> 68.1 us  [fused(): pl.pallas_call(fused_kernel, out_shape=(jax.ShapeDtypeStruct(tokens.shape...]
    reduce_scatter x2 -> x0, waiting for transfers between devices: 34 us -> none  [send_back(): lax.psum_scatter(partial_value.astype(jnp.bfloat16), 'dev', scatter_dimen...]
    all_gather x2 -> x0, blocking collectives: 28.9 us -> none  [deliver(): whole_rows = lax.all_gather(local_rows, 'dev', axis=1, tiled=True)]
    dot_general x12 -> x0, matrix products: 22.7 us -> none  [the longest x1 3.88 us: project_cotangent(): jnp.einsum('epf,hf->eph', portion, down_mat, preferred_element_type=jnp.f...]
    all_to_all x4 -> x0, starting transfers between devices: 15.1 us -> none  [the longest x2 7.81 us: deliver(): lax.all_to_all(build(whole_rows), 'node', split_axis=0, concat_axis=0, ti...]
    all_to_all x4 -> x0, waiting for transfers between devices: 13.7 us -> none  [the longest x2 7.91 us: deliver(): lax.all_to_all(build(whole_rows), 'node', split_axis=0, concat_axis=0, ti...]
    unnamed x8 -> x9, local copies, waits for them, and re-layouts: 2.48 us -> 6.27 us
  transfers between devices with their start and end apart: 6 -> 0, of which waited for: 4 -> 0; matrix products, arithmetic and copies ran while one was open for 15% -> 0% of each run, Pallas kernels for 0% -> 0%
where the time goes in v1:
time: 75.3 us; the launch traced here: 75 us
  Pallas kernels  68.1 us (90%)
  local copies, waits for them, and re-layouts  6.27 us (8%)
    pallas_call x1, Pallas kernels, fused(): pl.pallas_call(fused_kernel, out_shape=(jax.ShapeDtypeStruct(tokens.shape...  68.1 us
    unnamed x9, local copies, waits for them, and re-layouts  6.27 us

profile of v1, /device:TPU:0, one launch (start us, length us, event | category | flops | bytes accessed | tf_op | source)
XLA Modules:
  0.0 75.0 jit_solution(17070843891894938800)
XLA Ops:
  0.6 0.8 %copy.10.routes_in = s32[16,8]{1,0:T(8,128)S(1)} copy(s32[16,8]{0,1:T(8,128)} %param.8) | data formatting | bytes 1024 | tf_op args[1]
  1.4 0.8 %copy.11.codes_in = s32[16,8]{1,0:T(8,128)S(1)} copy(s32[16,8]{0,1:T(8,128)} %param.9) | data formatting | bytes 1024 | tf_op args[2]
  2.1 0.0 copy-start
  2.1 0.8 %copy-done = bf16[16,1024]{1,0:T(8,128)(2,1)S(1)} copy-done((bf16[16,1024]{1,0:T(8,128)(2,1)S(1)}, bf16[16,1024]{1,0:T(8,128)(2,1)}, u32[]{:S(2)}) %copy-start) | copy-done | bytes 32792
  2.9 0.0 copy-start.1
  2.9 0.8 %copy-done.1 = bf16[16,1024]{1,0:T(8,128)(2,1)S(1)} copy-done((bf16[16,1024]{1,0:T(8,128)(2,1)S(1)}, bf16[16,1024]{1,0:T(8,128)(2,1)}, u32[]{:S(2)}) %copy-start.1) | copy-done | bytes 32792
  3.7 68.1 %shard_map.94 = (bf16[16,1024]{1,0:T(8,128)(2,1)S(1)}, bf16[16,1024]{1,0:T(8,128)(2,1)S(1)}, bf16[1,512,4096]{2,1,0:T(8,128)(2,1)S(1)}) custom-call(bf16[16,1024]{1,0:T(8,128)(2,1)S(1)} %copy-done, s32[16,8]{1,0:T(8,128)S(1)} %copy.10.routes_in, s32[16,8]{1,0:T(8,128)S(1)} %copy.11.codes_in, bf16[1,4096,512]{2,1,0:T(8,128)(2,1)} %wg_in.1, ...), custom_call_target="tpu_custom_call" | custom-call | flops 3758096384 | bytes 16777216 | tf_op jit(solution)/shard_map/pallas_call | solution.py:291
  71.8 0.6 copy.15
  72.4 0.6 copy.16
  73.0 2.0 %copy.17 = bf16[1,512,4096]{2,1,0:T(8,128)(2,1)} copy(bf16[1,512,4096]{2,1,0:T(8,128)(2,1)S(1)} %get-tuple-element.8) | data formatting | bytes 8388608
Async XLA Ops:
  2.1 0.8 %copy-start = (bf16[16,1024]{1,0:T(8,128)(2,1)S(1)}, bf16[16,1024]{1,0:T(8,128)(2,1)}, u32[]{:S(2)}) copy-start(bf16[16,1024]{1,0:T(8,128)(2,1)} %tok_in.1) | copy-start | bytes 98308
  2.9 0.8 %copy-start.1 = (bf16[16,1024]{1,0:T(8,128)(2,1)S(1)}, bf16[16,1024]{1,0:T(8,128)(2,1)}, u32[]{:S(2)}) copy-start(bf16[16,1024]{1,0:T(8,128)(2,1)} %cot_in.1) | copy-start | bytes 98308

commit v2 on v1

--- a/solution.py
+++ b/solution.py
@@ -10,6 +10,7 @@
 MESH_IDS = pl.DeviceIdType.MESH
 ORDER_IN = (0, 1, 3, 2)
 ORDER_OUT = (2, 1, 3, 0)
+GROUP = 2
 
 
 def dot(a, b, a_dim=1, b_dim=0):
@@ -23,7 +24,7 @@
     layer_out, token_grad, down_out,
     x_all, gates, wg, wu, wd, gate_pre, up_pre, hid_grad, hidden, wcot, gate_grad, up_grad,
     part, r1, s1, r2, s2, r3, s3, r4, dgrad,
-    in_send, in_recv, g_send, g_recv, out_send, out_recv, w_sem, own_sem, d_sem,
+    in_send, in_recv, g_send, g_recv, out_send, out_recv, w_sem, own_sem, d_sem, named, codes,
 ):
     node, d = lax.axis_index("node"), lax.axis_index("dev")
     y, x, c = node // 4, (node // 2) % 2, node % 2
@@ -50,6 +51,16 @@
     peers = [(x_peer, d), (y_peer, d), (c_peer, d)] + [(node, (d + j) % 4) for j in (1, 2, 3)]
     for peer in peers:
         pl.semaphore_signal(barrier, inc=1, device_id=peer, device_id_type=MESH_IDS)
+
+    own = [
+        pltpu.make_async_copy(src, dst, own_sem.at[n])
+        for n, (src, dst) in enumerate((
+            (tok_in, x_all.at[0, 0, y, x, c]), (cot_in, x_all.at[1, 0, y, x, c]),
+            (routes_in, named), (codes_in, codes),
+        ))
+    ]
+    for copy in own:
+        copy.start()
 
     loads = {}
     for k in ORDER_IN:
@@ -62,24 +73,24 @@
     for load in loads.values():
         load.start()
 
+    for copy in own:
+        copy.wait()
     lane = lax.broadcasted_iota(jnp.int32, (tok_in.shape[0], 128), 1)
     table = jnp.zeros((tok_in.shape[0], 128), jnp.float32)
     for j in range(routes_in.shape[1]):
         table = table + jnp.where(
-            routes_in[:, j : j + 1] == lane,
-            codes_in[:, j : j + 1].astype(jnp.float32) / 65536.0,
+            named[:, j : j + 1] == lane,
+            codes[:, j : j + 1].astype(jnp.float32) / 65536.0,
             0.0,
         )
     gates[y, x, c] = table
-    x_all[0, 0, y, x, c] = tok_in[...]
-    x_all[1, 0, y, x, c] = cot_in[...]
 
     pl.semaphore_wait(barrier, 6)
 
     z_hop = {}
 
     def start_z(a):
-        own = tok_in if a == 0 else cot_in
+        own = x_all.at[a, 0, y, x, c]
         for j in (1, 3, 2):
             z_hop[a, 4 - j] = send(
                 own, x_all.at[a, 4 - j, y, x, c], in_send.at[a, j, 0], in_recv.at[a, 4 - j, 0],
@@ -222,31 +233,44 @@
 
     start_z(0)
     gates_stage(0)
-    for slot in range(18):
+    groups = 8 // GROUP
+    ready = groups // 2 + 2
+    last = ready + groups + 3
+
+    def members(group):
+        return range(group * GROUP, group * GROUP + GROUP) if 0 <= group < groups else ()
+
+    for slot in range(last):
         for stage in (3, 2, 1, 0):
-            if 0 <= slot - stage < 8:
-                gather_stage(slot - stage, stage)
+            for block in members(slot - stage):
+                gather_stage(block, stage)
         if slot == 0:
             start_z(1)
         if 1 <= slot <= 3:
             gates_stage(slot)
+        for block in members(slot - 3):
+            if block < 4:
+                project_in(block)
+        if slot == ready:
+            make_hidden()
+        for block in members(slot - ready):
+            if block < 4:
+                return_stage(block, 0)
+        for block in members(slot - 3):
+            if block >= 4:
+                project_cotangent(block - 4)
+        if slot == groups + 2:
+            make_grads()
+        for block in members(slot - ready):
+            if block >= 4:
+                return_stage(block, 0)
+        if slot >= last - 3:
+            for k in ((0, 1), (2,), (3,))[slot - (last - 3)]:
+                down_block(k)
         for stage in (3, 2, 1):
-            if 0 <= slot - 7 - stage < 8:
-                return_stage(slot - 7 - stage, stage)
-        if 3 <= slot <= 6:
-            project_in(slot - 3)
-        if slot == 6:
-            make_hidden()
-        if 7 <= slot <= 14:
-            return_stage(slot - 7, 0)
-        if 7 <= slot <= 10:
-            project_cotangent(slot - 7)
-        if slot == 10:
-            make_grads()
-        if slot >= 14:
-            down_block(slot - 14)
-        if slot == 15:
-            finish(0, layer_out)
+            for block in members(slot - ready - stage):
+                return_stage(block, stage)
+    finish(0, layer_out)
     finish(1, token_grad)
     for copy in sent:
         copy.wait_send()
@@ -285,7 +309,8 @@
         pltpu.VMEM((2, 4, here, width), low),
         pltpu.VMEM((4, hidden_width, width), low),
         dma((2, 4, 4)), dma((2, 4, 4)), dma((3,)), dma((3,)), dma((2, 4, 4)), dma((2, 4, 4)),
-        dma((3, 4)), dma((2,)), dma((4,)),
+        dma((3, 4)), dma((4,)), dma((4,)),
+        pltpu.VMEM(routes.shape, jnp.int32), pltpu.VMEM(gate_codes.shape, jnp.int32),
     ]
     flops = 2 * 7 * rows * 4 * width * hidden_width
     return pl.pallas_call(
@@ -295,7 +320,7 @@
             jax.ShapeDtypeStruct(tokens.shape, low),
             jax.ShapeDtypeStruct(w_down.shape, low),
         ),
-        in_specs=[vmem, vmem, vmem, anywhere, anywhere, anywhere, vmem],
+        in_specs=[anywhere] * 7,
         out_specs=(vmem, vmem, anywhere),
         scratch_shapes=scratch,
         compiler_params=pltpu.CompilerParams(

time: 75.3 us -> 58.5 us (0.78)
  Pallas kernels: 68.1 us -> 51.3 us
    pallas_call x1, Pallas kernels: 68.1 us -> 51.3 us  [fused(): pl.pallas_call(fused_kernel, out_shape=(jax.ShapeDtypeStruct(tokens.shape...]
where the time goes in v2:
time: 58.5 us; the launch traced here: 58.2 us
  Pallas kernels  51.3 us (88%)
  local copies, waits for them, and re-layouts  6.27 us (11%)
  between operations  0.64 us (1%)
    pallas_call x1, Pallas kernels, fused(): pl.pallas_call(fused_kernel, out_shape=(jax.ShapeDtypeStruct(tokens.shape...  51.3 us
    unnamed x9, local copies, waits for them, and re-layouts  6.27 us

profile of v2, /device:TPU:0, one launch (start us, length us, event | category | flops | bytes accessed | tf_op | source)
XLA Modules:
  0.0 58.2 jit_solution(15949612285251090416)
XLA Ops:
  0.6 0.8 %copy.10.routes_in = s32[16,8]{1,0:T(8,128)S(1)} copy(s32[16,8]{0,1:T(8,128)} %param.8) | data formatting | bytes 1024 | tf_op args[1]
  1.4 0.8 %copy.11.codes_in = s32[16,8]{1,0:T(8,128)S(1)} copy(s32[16,8]{0,1:T(8,128)} %param.9) | data formatting | bytes 1024 | tf_op args[2]
  2.1 0.0 copy-start
  2.1 0.8 %copy-done = bf16[16,1024]{1,0:T(8,128)(2,1)S(1)} copy-done((bf16[16,1024]{1,0:T(8,128)(2,1)S(1)}, bf16[16,1024]{1,0:T(8,128)(2,1)}, u32[]{:S(2)}) %copy-start) | copy-done | bytes 32792
  2.9 0.0 copy-start.1
  2.9 0.8 %copy-done.1 = bf16[16,1024]{1,0:T(8,128)(2,1)S(1)} copy-done((bf16[16,1024]{1,0:T(8,128)(2,1)S(1)}, bf16[16,1024]{1,0:T(8,128)(2,1)}, u32[]{:S(2)}) %copy-start.1) | copy-done | bytes 32792
  3.7 51.3 %shard_map.94 = (bf16[16,1024]{1,0:T(8,128)(2,1)S(1)}, bf16[16,1024]{1,0:T(8,128)(2,1)S(1)}, bf16[1,512,4096]{2,1,0:T(8,128)(2,1)S(1)}) custom-call(bf16[16,1024]{1,0:T(8,128)(2,1)S(1)} %copy-done, s32[16,8]{1,0:T(8,128)S(1)} %copy.10.routes_in, s32[16,8]{1,0:T(8,128)S(1)} %copy.11.codes_in, bf16[1,4096,512]{2,1,0:T(8,128)(2,1)} %wg_in.1, ...), custom_call_target="tpu_custom_call" | custom-call | flops 3758096384 | bytes 16777216 | tf_op jit(solution)/shard_map/pallas_call | solution.py:316
  54.9 0.6 %copy.15 = bf16[16,1024]{1,0:T(8,128)(2,1)} copy(bf16[16,1024]{1,0:T(8,128)(2,1)S(1)} %get-tuple-element.6) | data formatting | bytes 65536
  55.6 0.6 %copy.16 = bf16[16,1024]{1,0:T(8,128)(2,1)} copy(bf16[16,1024]{1,0:T(8,128)(2,1)S(1)} %get-tuple-element.7) | data formatting | bytes 65536
  56.2 2.0 %copy.17 = bf16[1,512,4096]{2,1,0:T(8,128)(2,1)} copy(bf16[1,512,4096]{2,1,0:T(8,128)(2,1)S(1)} %get-tuple-element.8) | data formatting | bytes 8388608
Async XLA Ops:
  2.1 0.8 %copy-start = (bf16[16,1024]{1,0:T(8,128)(2,1)S(1)}, bf16[16,1024]{1,0:T(8,128)(2,1)}, u32[]{:S(2)}) copy-start(bf16[16,1024]{1,0:T(8,128)(2,1)} %tok_in.1) | copy-start | bytes 98308
  2.9 0.8 %copy-start.1 = (bf16[16,1024]{1,0:T(8,128)(2,1)S(1)}, bf16[16,1024]{1,0:T(8,128)(2,1)}, u32[]{:S(2)}) copy-start(bf16[16,1024]{1,0:T(8,128)(2,1)} %cot_in.1) | copy-start | bytes 98308

commit v3 on v2

--- a/solution.py
+++ b/solution.py
@@ -10,7 +10,7 @@
 MESH_IDS = pl.DeviceIdType.MESH
 ORDER_IN = (0, 1, 3, 2)
 ORDER_OUT = (2, 1, 3, 0)
-GROUP = 2
+GROUP = 4
 
 
 def dot(a, b, a_dim=1, b_dim=0):
@@ -20,19 +20,19 @@
 
 
 def fused_kernel(
-    tok_in, routes_in, codes_in, wg_in, wu_in, wd_in, cot_in,
+    pair_in, named_in, wg_in, wu_in, wd_in,
     layer_out, token_grad, down_out,
     x_all, gates, wg, wu, wd, gate_pre, up_pre, hid_grad, hidden, wcot, gate_grad, up_grad,
     part, r1, s1, r2, s2, r3, s3, r4, dgrad,
-    in_send, in_recv, g_send, g_recv, out_send, out_recv, w_sem, own_sem, d_sem, named, codes,
+    in_send, in_recv, g_send, g_recv, out_send, out_recv, w_sem, own_sem, d_sem, named,
 ):
     node, d = lax.axis_index("node"), lax.axis_index("dev")
     y, x, c = node // 4, (node // 2) % 2, node % 2
     x_peer = (y * 2 + 1 - x) * 2 + c
     y_peer = ((1 - y) * 2 + x) * 2 + c
     c_peer = (y * 2 + x) * 2 + 1 - c
-    width = tok_in.shape[1]
-    rows = 8 * tok_in.shape[0]
+    width = pair_in.shape[2]
+    rows = 8 * pair_in.shape[1]
     sent = []
 
     def send(src, dst, send_sem, recv_sem, target):
@@ -55,8 +55,8 @@
     own = [
         pltpu.make_async_copy(src, dst, own_sem.at[n])
         for n, (src, dst) in enumerate((
-            (tok_in, x_all.at[0, 0, y, x, c]), (cot_in, x_all.at[1, 0, y, x, c]),
-            (routes_in, named), (codes_in, codes),
+            (pair_in.at[0], x_all.at[0, 0, y, x, c]), (pair_in.at[1], x_all.at[1, 0, y, x, c]),
+            (named_in, named),
         ))
     ]
     for copy in own:
@@ -72,18 +72,18 @@
         )
     for load in loads.values():
         load.start()
-
     for copy in own:
         copy.wait()
-    lane = lax.broadcasted_iota(jnp.int32, (tok_in.shape[0], 128), 1)
-    table = jnp.zeros((tok_in.shape[0], 128), jnp.float32)
-    for j in range(routes_in.shape[1]):
-        table = table + jnp.where(
-            named[:, j : j + 1] == lane,
-            codes[:, j : j + 1].astype(jnp.float32) / 65536.0,
-            0.0,
-        )
+
+    here, choices = pair_in.shape[1], 8
+    columns = named[...].T
+    lane = lax.broadcasted_iota(jnp.int32, (here, 128), 1).astype(jnp.float32)
+    table = jnp.zeros((here, 128), jnp.float32)
+    for j in range(choices):
+        weight = columns[:here, choices + j : choices + j + 1] / 65536.0
+        table = table + jnp.where(columns[:here, j : j + 1] == lane, weight, 0.0)
     gates[y, x, c] = table
+
 
     pl.semaphore_wait(barrier, 6)
 
@@ -309,9 +309,11 @@
         pltpu.VMEM((2, 4, here, width), low),
         pltpu.VMEM((4, hidden_width, width), low),
         dma((2, 4, 4)), dma((2, 4, 4)), dma((3,)), dma((3,)), dma((2, 4, 4)), dma((2, 4, 4)),
-        dma((3, 4)), dma((4,)), dma((4,)),
-        pltpu.VMEM(routes.shape, jnp.int32), pltpu.VMEM(gate_codes.shape, jnp.int32),
+        dma((3, 4)), dma((3,)), dma((4,)),
+        pltpu.VMEM((128, 128), full),
     ]
+    named = jnp.concatenate([routes.T, gate_codes.T], axis=0).astype(full)
+    named = jnp.pad(named, ((0, 128 - named.shape[0]), (0, 128 - here)))
     flops = 2 * 7 * rows * 4 * width * hidden_width
     return pl.pallas_call(
         fused_kernel,
@@ -320,7 +322,7 @@
             jax.ShapeDtypeStruct(tokens.shape, low),
             jax.ShapeDtypeStruct(w_down.shape, low),
         ),
-        in_specs=[anywhere] * 7,
+        in_specs=[anywhere] * 5,
         out_specs=(vmem, vmem, anywhere),
         scratch_shapes=scratch,
         compiler_params=pltpu.CompilerParams(
@@ -329,7 +331,7 @@
         cost_estimate=pl.CostEstimate(
             flops=flops, bytes_accessed=8 * w_gate.size, transcendentals=2 * rows * hidden_width
         ),
-    )(tokens, routes, gate_codes, w_gate, w_up, w_down, cotangent)
+    )(jnp.stack([tokens, cotangent]), named, w_gate, w_up, w_down)
 
 
 exact_mode = lax.Precision.HIGHEST

time: 58.5 us -> 53.5 us (0.915)
  Pallas kernels: 51.3 us -> 47.9 us
  local copies, waits for them, and re-layouts: 6.27 us -> 3.25 us
  other arithmetic: 0 us -> 1.49 us
    pallas_call x1, Pallas kernels: 51.3 us -> 47.9 us  [fused(): pl.pallas_call(fused_kernel, out_shape=(jax.ShapeDtypeStruct(tokens.shape...]
    unnamed x9 -> x3, local copies, waits for them, and re-layouts: 6.27 us -> 3.24 us
    another operation x0 -> x1, other arithmetic: none -> 0.78 us  [fused(): jnp.stack([tokens, cotangent])]
    convert_element_type x0 -> x1, other arithmetic: none -> 0.71 us  [fused(): named = jnp.concatenate([routes.T, gate_codes.T], axis=0).astype(full)]
where the time goes in v3:
time: 53.5 us; the launch traced here: 53.3 us
  Pallas kernels  47.9 us (90%)
  local copies, waits for them, and re-layouts  3.25 us (6%)
  other arithmetic  1.49 us (3%)
  between operations  0.64 us (1%)
    pallas_call x1, Pallas kernels, fused(): pl.pallas_call(fused_kernel, out_shape=(jax.ShapeDtypeStruct(tokens.shape...  47.9 us
    unnamed x3, local copies, waits for them, and re-layouts  3.24 us

profile of v3, /device:TPU:0, one launch (start us, length us, event | category | flops | bytes accessed | tf_op | source)
XLA Modules:
  0.0 53.3 jit_solution(6572371154587764951)
XLA Ops:
  0.6 0.7 %add_convert_fusion = f32[16,16]{1,0:T(8,128)S(1)} fusion(s32[8,16]{1,0:T(8,128)} %bitcast.6, s32[8,16]{1,0:T(8,128)} %bitcast.7), kind=kLoop, calls=%fused_computation.1 | loop fusion | flops 512 | bytes 2048 | tf_op jit(solution)/shard_map/convert_element_type | solution.py:315
  1.3 0.8 %pad_maximum_fusion.pair_in = bf16[2,16,1024]{2,1,0:T(8,128)(2,1)S(1)} fusion(bf16[1,16,1024]{2,1,0:T(8,128)(2,1)} %bitcast.4, bf16[1,16,1024]{2,1,0:T(8,128)(2,1)} %bitcast.5), kind=kLoop, calls=%fused_computation | loop fusion | flops 32768 | bytes 131072 | tf_op jit(solution)/shard_map/stack | solution.py:334
  2.1 47.9 %shard_map.94 = (bf16[16,1024]{1,0:T(8,128)(2,1)S(1)}, bf16[16,1024]{1,0:T(8,128)(2,1)S(1)}, bf16[1,512,4096]{2,1,0:T(8,128)(2,1)S(1)}) custom-call(bf16[2,16,1024]{2,1,0:T(8,128)(2,1)S(1)} %pad_maximum_fusion.pair_in, f32[128,128]{1,0:T(8,128)S(1)} %pad.4.named_in, bf16[1,4096,512]{2,1,0:T(8,128)(2,1)} %wg_in.1, bf16[1,4096,512]{2,1,0:T(8,128)(2,1)} %wu_in.1, ...), custom_call_target="tpu_custom_call" | custom-call | flops 3758096384 | bytes 16777216 | tf_op jit(solution)/shard_map/pallas_call | solution.py:318
  50.0 0.6 %copy.13 = bf16[16,1024]{1,0:T(8,128)(2,1)} copy(bf16[16,1024]{1,0:T(8,128)(2,1)S(1)} %get-tuple-element.6) | data formatting | bytes 65536
  50.7 0.6 %copy.14 = bf16[16,1024]{1,0:T(8,128)(2,1)} copy(bf16[16,1024]{1,0:T(8,128)(2,1)S(1)} %get-tuple-element.7) | data formatting | bytes 65536
  51.3 2.0 %copy.15 = bf16[1,512,4096]{2,1,0:T(8,128)(2,1)} copy(bf16[1,512,4096]{2,1,0:T(8,128)(2,1)S(1)} %get-tuple-element.8) | data formatting | bytes 8388608
  (1 shorter events, 0.0 us)

commit v4 on v3

--- a/solution.py
+++ b/solution.py
@@ -261,15 +261,24 @@
                 project_cotangent(block - 4)
         if slot == groups + 2:
             make_grads()
+        early = slot == ready + 1
+        for block in range(4 if early else 0):
+            return_stage(block, 1)
         for block in members(slot - ready):
             if block >= 4:
                 return_stage(block, 0)
+        for block in range(4 if early else 0):
+            return_stage(block, 2)
         if slot >= last - 3:
             for k in ((0, 1), (2,), (3,))[slot - (last - 3)]:
                 down_block(k)
         for stage in (3, 2, 1):
             for block in members(slot - ready - stage):
-                return_stage(block, stage)
+                if block >= 4:
+                    return_stage(block, stage)
+        if slot == last - 2:
+            for block in range(4):
+                return_stage(block, 3)
     finish(0, layer_out)
     finish(1, token_grad)
     for copy in sent:

time: 53.5 us -> 50.4 us (0.942)
  Pallas kernels: 47.9 us -> 44.8 us
    pallas_call x1, Pallas kernels: 47.9 us -> 44.8 us  [fused(): pl.pallas_call(fused_kernel, out_shape=(jax.ShapeDtypeStruct(tokens.shape...]
where the time goes in v4:
time: 50.4 us; the launch traced here: 50.2 us
  Pallas kernels  44.8 us (89%)
  local copies, waits for them, and re-layouts  3.25 us (6%)
  other arithmetic  1.49 us (3%)
  between operations  0.64 us (1%)
    pallas_call x1, Pallas kernels, fused(): pl.pallas_call(fused_kernel, out_shape=(jax.ShapeDtypeStruct(tokens.shape...  44.8 us
    unnamed x3, local copies, waits for them, and re-layouts  3.24 us

profile of v4, /device:TPU:0, one launch (start us, length us, event | category | flops | bytes accessed | tf_op | source)
XLA Modules:
  0.0 50.2 jit_solution(16546459139544379453)
XLA Ops:
  0.6 0.7 %add_convert_fusion = f32[16,16]{1,0:T(8,128)S(1)} fusion(s32[8,16]{1,0:T(8,128)} %bitcast.6, s32[8,16]{1,0:T(8,128)} %bitcast.7), kind=kLoop, calls=%fused_computation.1 | loop fusion | flops 512 | bytes 2048 | tf_op jit(solution)/shard_map/convert_element_type | solution.py:324
  1.3 0.8 %pad_maximum_fusion.pair_in = bf16[2,16,1024]{2,1,0:T(8,128)(2,1)S(1)} fusion(bf16[1,16,1024]{2,1,0:T(8,128)(2,1)} %bitcast.4, bf16[1,16,1024]{2,1,0:T(8,128)(2,1)} %bitcast.5), kind=kLoop, calls=%fused_computation | loop fusion | flops 32768 | bytes 131072 | tf_op jit(solution)/shard_map/stack | solution.py:343
  2.1 44.8 %shard_map.94 = (bf16[16,1024]{1,0:T(8,128)(2,1)S(1)}, bf16[16,1024]{1,0:T(8,128)(2,1)S(1)}, bf16[1,512,4096]{2,1,0:T(8,128)(2,1)S(1)}) custom-call(bf16[2,16,1024]{2,1,0:T(8,128)(2,1)S(1)} %pad_maximum_fusion.pair_in, f32[128,128]{1,0:T(8,128)S(1)} %pad.4.named_in, bf16[1,4096,512]{2,1,0:T(8,128)(2,1)} %wg_in.1, bf16[1,4096,512]{2,1,0:T(8,128)(2,1)} %wu_in.1, ...), custom_call_target="tpu_custom_call" | custom-call | flops 3758096384 | bytes 16777216 | tf_op jit(solution)/shard_map/pallas_call | solution.py:327
  46.9 0.6 %copy.13 = bf16[16,1024]{1,0:T(8,128)(2,1)} copy(bf16[16,1024]{1,0:T(8,128)(2,1)S(1)} %get-tuple-element.6) | data formatting | bytes 65536
  47.5 0.6 %copy.14 = bf16[16,1024]{1,0:T(8,128)(2,1)} copy(bf16[16,1024]{1,0:T(8,128)(2,1)S(1)} %get-tuple-element.7) | data formatting | bytes 65536
  48.1 2.0 %copy.15 = bf16[1,512,4096]{2,1,0:T(8,128)(2,1)} copy(bf16[1,512,4096]{2,1,0:T(8,128)(2,1)S(1)} %get-tuple-element.8) | data formatting | bytes 8388608
  (1 shorter events, 0.0 us)
